TPU v7x, 512 devices: a whole 4x8x8 slice. The times are simulated.
512 devices in a mesh: leaf: 8 (over y), row: 8 (over z_hi, x), col: 8 (over z_lo, core).
Axes of the slice: x: 4, y: 8, z: 8 (z_hi: 2, z_lo: 4; z = z_hi * 4 + z_lo), core: 2. Of those that a mesh axis runs over, the one named last changes fastest.
Arguments:
- parent_front: float32 [2, 1, 8192, 8, 1024], P(None, None, ('leaf', 'row'), None, 'col'), as said below
- child_updates: float32 [2, 1, 8192, 4, 1024], P(None, None, ('leaf', 'row'), None, 'col')
- child_map: int32 [2, 32], replicated, may hold values from 0 to 63, as said below
Outputs:
- factored_front: float32 [2, 1, 8192, 8, 1024], P(None, None, ('leaf', 'row'), None, 'col')
Inputs may be any that keep to these rules, and one draw needn't show every extreme that they name: For each child c the entries child_map[c, :] are distinct, child_map[c, a] leaves the same remainder modulo 8 as a, and each child's map contains the first and the last parent block of every remainder class. Each row of the parent front's pivot block has a diagonal entry whose magnitude exceeds the norm of the row's other entries in that block; parent_front and child_updates are complex symmetric.
All inputs are finite; a program needn't handle non-finite values.
Results may differ from a plain program's by a relative error of at most 0.0015.
Values may be sent and summed in bfloat16 or wider, within the bound.
No kernel may reach another device: no remote copies, remote signals or barrier semaphores. Data moves between devices by JAX's collectives and lax.ppermute only.
A program may use at most 64 MiB of HBM per device.

v0:
```python
import jax
import jax.numpy as jnp
from jax import lax
from jax.sharding import PartitionSpec as P

NS_STEPS = 3


def spread(value, axis, source):
    kept = jnp.where(lax.axis_index(axis) == source, value, 0).astype(value.dtype)
    return lax.psum(kept, axis)


def complex_product(left, right):
    real_part = jnp.matmul(left[0], right[0], precision=lax.Precision.HIGHEST) - jnp.matmul(
        left[1], right[1], precision=lax.Precision.HIGHEST
    )
    imag_part = jnp.matmul(left[0], right[1], precision=lax.Precision.HIGHEST) + jnp.matmul(
        left[1], right[0], precision=lax.Precision.HIGHEST
    )
    return jnp.stack([real_part, imag_part])


def transposed_product(left, right):
    real_part = jnp.einsum(
        "rp,cp->rc", left[0], right[0], preferred_element_type=jnp.float32
    ) - jnp.einsum("rp,cp->rc", left[1], right[1], preferred_element_type=jnp.float32)
    imag_part = jnp.einsum(
        "rp,cp->rc", left[0], right[1], preferred_element_type=jnp.float32
    ) + jnp.einsum("rp,cp->rc", left[1], right[0], preferred_element_type=jnp.float32)
    return jnp.stack([real_part, imag_part])


def newton_inverse(pivot_block):
    diag_real = jnp.diagonal(pivot_block[0])
    diag_imag = jnp.diagonal(pivot_block[1])
    denominator = diag_real * diag_real + diag_imag * diag_imag
    current = jnp.stack([jnp.diag(diag_real / denominator), jnp.diag(-diag_imag / denominator)])
    for newton_step in range(NS_STEPS):
        product = complex_product(pivot_block, current)
        current = 2.0 * current - complex_product(current, product)
    return current


def local(parent_front, child_updates, child_map):
    leaf_count = lax.axis_size("leaf")
    row_count = lax.axis_size("row")
    col_count = lax.axis_size("col")
    rank_count = leaf_count * row_count
    half_ranks = rank_count // 2
    my_row = lax.axis_index("row")
    my_col = lax.axis_index("col")
    my_rank = lax.axis_index("leaf") * row_count + my_row
    row_blocks = parent_front.shape[1]
    block_size = parent_front.shape[2]
    local_cols = parent_front.shape[3]
    child_rows = child_updates.shape[1]
    child_cols = child_updates.shape[3]
    child_order = child_map.shape[1]
    panel_width = 2 * block_size
    flat_map = child_map.reshape(-1)
    pieces = lax.all_gather(child_updates[None], "leaf", axis=0, tiled=True)
    senders = pieces.shape[0]
    source_leaf = jnp.arange(senders, dtype=jnp.int32)
    source_rank = source_leaf * row_count + my_row
    source_child = source_rank // half_ranks
    source_slot = source_rank % half_ranks
    child_block = (
        jnp.arange(child_rows, dtype=jnp.int32)[None, :] * half_ranks + source_slot[:, None]
    )
    target_rows = jnp.take(flat_map, source_child[:, None] * child_order + child_block)
    local_index = jnp.arange(row_blocks, dtype=jnp.int32)
    row_select = (
        (target_rows[:, :, None] % rank_count == my_rank)
        & (target_rows[:, :, None] // rank_count == local_index[None, None, :])
    ).astype(jnp.float32)
    column_block = jnp.arange(child_cols, dtype=jnp.int32) * col_count + my_col
    target_cols = jnp.take(flat_map, source_child[:, None] * child_order + column_block[None, :])
    col_select = (
        target_cols[:, :, None] // col_count
        == jnp.arange(local_cols, dtype=jnp.int32)[None, None, :]
    ).astype(jnp.float32)
    added = jnp.einsum(
        "ntu,nztxby,nbs->zuxsy", row_select, pieces, col_select, precision=lax.Precision.HIGHEST
    )
    assembled = parent_front + added
    first_block = assembled[:, :, :, 0, :]
    columns = [spread(first_block, "col", owner) for owner in range(2)]
    panel_rows = jnp.concatenate(columns, axis=3)
    pivot_parts = [
        spread(panel_rows[:, 0].astype(jnp.bfloat16), ("leaf", "row"), owner).astype(jnp.float32)
        for owner in range(2)
    ]
    pivot_block = jnp.concatenate(pivot_parts, axis=1)
    inverse = newton_inverse(pivot_block)
    multipliers = complex_product(
        panel_rows.reshape(2, row_blocks * block_size, panel_width), inverse
    )
    compact = panel_rows.astype(jnp.bfloat16)
    gathered = lax.all_gather(compact, ("leaf", "row"), axis=2, tiled=True)
    gathered = gathered.reshape(
        2, row_blocks, rank_count // col_count, col_count, block_size, panel_width
    )
    gathered = lax.dynamic_index_in_dim(gathered, my_col, axis=3, keepdims=False)
    column_panel = gathered.reshape(2, local_cols * block_size, panel_width)
    update_all = transposed_product(multipliers.astype(jnp.bfloat16), column_panel)
    schur_part = assembled - update_all.reshape(assembled.shape)
    column_start = jnp.minimum(my_col, 1) * block_size
    mult_piece = lax.dynamic_slice_in_dim(multipliers, column_start, block_size, axis=2)
    mult_piece = mult_piece.reshape(2, row_blocks, block_size, 1, block_size)
    global_row = jnp.arange(row_blocks, dtype=jnp.int32) * rank_count + my_rank
    global_col = jnp.arange(local_cols, dtype=jnp.int32) * col_count + my_col
    pivot_row = (global_row < 2)[None, :, None, None, None]
    panel_col = (global_col < 2)[None, None, None, :, None]
    return jnp.where(pivot_row, assembled, jnp.where(panel_col, mult_piece, schur_part))


def solution(mesh):
    in_specs = (
        P(None, None, ("leaf", "row"), None, "col"),
        P(None, None, ("leaf", "row"), None, "col"),
        P(),
    )
    out_specs = P(None, None, ("leaf", "row"), None, "col")
    return jax.shard_map(local, mesh=mesh, in_specs=in_specs, out_specs=out_specs, check_vma=False)
```

profile of v0, /device:TPU:2, one launch (start us, length us, event | category | flops | bytes accessed | tf_op | source)
XLA Modules:
  0.0 1166.9 jit_solution(15491226585552927433)
XLA Ops:
  6.5 2.0 copy.17
  8.8 0.8 reshape.505
  9.6 0.7 gather_fusion
  10.5 0.7 gather_fusion.1
  11.2 60.0 %all-gather.6.cloned.1.call-done = f32[16,1,128,4,128]{4,2,3,1,0:T(8,128)} async-done(((f32[2,1,128,4,128]{4,2,3,1,0:T(8,128)}), f32[16,1,128,4,128]{4,2,3,1,0:T(8,128)}) %all-gather.6.cloned.1.call-update) | async-done | bytes 4194320 | tf_op jit(solution)/shard_map/all_gather | solution.py:62
  71.2 11.3 fusion.5
  82.6 0.8 broadcast_select_fusion
  83.4 0.7 select_bitcast_fusion.2
  84.1 75.9 %all-reduce.5.cloned.1.call-done = (f32[2,1,128,128]{3,2,0,1:T(8,128)}, f32[2,1,128,128]{3,2,0,1:T(8,128)}) async-done(((f32[2,1,128,128]{3,2,0,1:T(8,128)}, f32[2,1,128,128]{3,2,0,1:T(8,128)}), (f32[2,1,128,128]{3,2,0,1:T(8,128)}, f32[2,1,128,128]{3,2,0,1:T(8,128)})) %all-reduce.5.cloned.1.call-update) | async-done | bytes 262160 | tf_op jit(solution)/shard_map/psum | solution.py:11
  160.0 0.9 constant_dynamic-update-slice_fusion.1
  161.0 0.9 constant_dynamic-update-slice_fusion
  161.9 0.7 select_bitcast_fusion
  162.6 0.7 select_bitcast_fusion.1
  163.5 0.3 all-gather.4.cloned.1.call-update
  163.9 785.1 %all-reduce.7.cloned.1.call-done = (bf16[2,128,256]{2,1,0:T(8,128)(2,1)}, bf16[2,128,256]{2,1,0:T(8,128)(2,1)}) async-done(((bf16[2,128,256]{2,1,0:T(8,128)(2,1)}, bf16[2,128,256]{2,1,0:T(8,128)(2,1)}), (bf16[2,128,256]{2,1,0:T(8,128)(2,1)}, bf16[2,128,256]{2,1,0:T(8,128)(2,1)})) %all-reduce.7.cloned.1.call-update) | async-done | bytes 262160 | tf_op jit(solution)/shard_map/psum | solution.py:11
  949.0 0.9 constant_dynamic-update-slice_fusion.3
  949.9 0.9 constant_dynamic-update-slice_fusion.2
  951.0 2.3 gather_fusion.2
  953.3 2.3 gather_fusion.3
  955.7 0.3 fusion.32
  956.0 0.4 fusion.24
  956.4 0.3 convolution_subtract_fusion.6
  956.7 0.4 fusion.30
  957.2 0.3 convolution_add_fusion.6
  957.5 0.4 fusion.15
  957.9 0.4 fusion.27
  958.4 0.4 fusion.14
  959.1 0.3 fusion.41
  959.7 0.3 convolution_subtract_fusion.4
  960.0 0.4 fusion.40
  960.4 0.3 convolution_add_fusion.4
  960.7 0.4 fusion.13
  961.1 0.4 fusion.39
  961.5 0.4 fusion.12
  962.0 0.3 fusion.45
  962.3 0.3 fusion.46
  962.6 0.3 convolution_subtract_fusion.2
  962.9 0.4 fusion.44
  963.3 0.3 convolution_add_fusion.2
  963.6 0.4 fusion.11
  964.0 0.4 fusion.43
  964.4 0.4 fusion.10
  966.1 190.3 %all-gather.4.cloned.1.call-done = bf16[2,1,8192,256]{3,2,0,1:T(8,128)(2,1)} async-done(((bf16[2,1,128,256]{3,2,0,1:T(8,128)(2,1)}), bf16[2,1,8192,256]{3,2,0,1:T(8,128)(2,1)}) %all-gather.4.cloned.1.call-update) | async-done | bytes 8388624 | tf_op jit(solution)/shard_map/all_gather | solution.py:100
  1156.4 1.3 constant_dynamic-slice_fusion
  1158.0 0.3 fusion.64
  1158.3 0.3 fusion.9
  1158.7 0.3 fusion.8
  1159.1 1.2 fusion.20
  (42 shorter events, 3.4 us)
Async XLA Ops:
  6.5 64.7 %copy-start.1 = (f32[2,1,128,8,128]{4,3,2,1,0:T(8,128)S(1)}, f32[2,1,128,8,128]{4,3,2,1,0:T(8,128)}, u32[]{:S(2)}) copy-start(f32[2,1,128,8,128]{4,3,2,1,0:T(8,128)} %param.3) | copy-start | bytes 3145732
  6.5 64.7 %all-gather.6.cloned.1.call-start = ((), (), s32[]{:S(2)}) async-start(), calls=%async_computation.1 | async-start | bytes 4718592 | tf_op jit(solution)/shard_map/all_gather | solution.py:62
  8.5 151.5 %all-reduce.5.cloned.1.call-start = ((), (), s32[]{:S(2)}) async-start(), calls=%async_computation.2 | async-start | bytes 524288 | tf_op jit(solution)/shard_map/psum | solution.py:11
  84.1 864.9 %all-reduce.7.cloned.1.call-start = ((), (), s32[]{:S(2)}) async-start(), calls=%async_computation.3 | async-start | bytes 524288 | tf_op jit(solution)/shard_map/psum | solution.py:11
  162.5 1.0 copy-start
  163.3 993.1 %all-gather.4.cloned.1.call-start = ((), (), s32[]{:S(2)}) async-start(), calls=%async_computation | async-start | bytes 8519680 | tf_op jit(solution)/shard_map/all_gather | solution.py:100
Sparse Core Ops, SparseCore 0:
  9.4 61.7 all-gather.5
  84.2 75.7 all-reduce.4
  163.4 785.5 all-reduce.6
  953.3 203.0 all-gather.3
where the time goes:
time: 1170 us
  waiting for transfers between devices  1110 us (95%)
  matrix products  22.2 us (2%)
  local copies, waits for them, and re-layouts  14.2 us (1%)
  between operations  13.6 us (1%)
    psum x2, waiting for transfers between devices, spread(): return lax.psum(kept, axis)  861 us
    all_gather x1, waiting for transfers between devices, local(): gathered = lax.all_gather(compact, ('leaf', 'row'), axis=2, tiled=True)  190 us
    all_gather x1, waiting for transfers between devices, local(): pieces = lax.all_gather(child_updates[None], 'leaf', axis=0, tiled=True)  60 us
  transfers between devices with their start and end apart: 4, of which 4 were waited for; matrix products, arithmetic and copies ran while one was open for 2% of the time, Pallas kernels for 0%

commit v1 on v0

--- a/solution.py
+++ b/solution.py
@@ -6,9 +6,13 @@
 NS_STEPS = 3
 
 
+def place_tiles_all(x0, mesh_name):
+    return lax.all_gather(x0, axis_name=mesh_name).sum(axis=0)
+
+
 def spread(value, axis, source):
     kept = jnp.where(lax.axis_index(axis) == source, value, 0).astype(value.dtype)
-    return lax.psum(kept, axis)
+    return place_tiles_all(kept, mesh_name=axis)
 
 
 def complex_product(left, right):

time: 1170 us -> 778 us (0.66)
  waiting for transfers between devices: 1110 us -> 715 us
    psum x2 -> x0, waiting for transfers between devices: 861 us -> none  [spread(): return lax.psum(kept, axis)]
    all_gather x0 -> x4, waiting for transfers between devices: none -> 473 us  [place_tiles_all(): return lax.all_gather(x0, axis_name=mesh_name).sum(axis=0)]
    reduce_sum x0 -> x4, other arithmetic: none -> 11.7 us  [place_tiles_all(): return lax.all_gather(x0, axis_name=mesh_name).sum(axis=0)]
  transfers between devices with their start and end apart: 4 -> 6, of which waited for: 4 -> 6; matrix products, arithmetic and copies ran while one was open for 2% -> 4% of each run, Pallas kernels for 0% -> 0%
where the time goes in v1:
time: 778 us
  waiting for transfers between devices  715 us (92%)
  matrix products  22.2 us (3%)
  other arithmetic  16 us (2%)
  between operations  13.9 us (2%)
  local copies, waits for them, and re-layouts  10.4 us (1%)
    all_gather x4, waiting for transfers between devices, place_tiles_all(): return lax.all_gather(x0, axis_name=mesh_name).sum(axis=0)  473 us
    all_gather x1, waiting for transfers between devices, local(): gathered = lax.all_gather(compact, ('leaf', 'row'), axis=2, tiled=True)  181 us
    all_gather x1, waiting for transfers between devices, local(): pieces = lax.all_gather(child_updates[None], 'leaf', axis=0, tiled=True)  60.1 us
  transfers between devices with their start and end apart: 6, of which 6 were waited for; matrix products, arithmetic and copies ran while one was open for 4% of the time, Pallas kernels for 0%

profile of v1, /device:TPU:2, one launch (start us, length us, event | category | flops | bytes accessed | tf_op | source)
XLA Modules:
  0.0 777.8 jit_solution(18082903246671114510)
XLA Ops:
  6.5 1.9 copy.13
  8.7 0.8 reshape.537
  9.4 0.7 gather_fusion
  10.4 0.6 gather_fusion.1
  11.1 60.1 %all-gather.14.cloned.1.call-done = f32[16,1,128,4,128]{4,2,3,1,0:T(8,128)} async-done(((f32[2,1,128,4,128]{4,2,3,1,0:T(8,128)}), f32[16,1,128,4,128]{4,2,3,1,0:T(8,128)}) %all-gather.14.cloned.1.call-update) | async-done | bytes 4194320 | tf_op jit(solution)/shard_map/all_gather | solution.py:66
  71.2 11.3 %fusion.5 = f32[2,1,128,8,128]{4,3,2,0,1:T(8,128)S(1)} fusion(f32[8,2,128,4,128]{4,2,3,1,0:T(8,128)} %bitcast.166, f32[2,1,128,8,128]{4,3,2,1,0:T(8,128)} %param.3, f32[8]{0:T(128)S(1)} %and_convert_fusion, s32[8,4]{0,1:T(4,128)S(1)} %copy.12), kind=kOutput, calls=%fused_computation.9 | convolution fusion | flops 100925952 | bytes 6291616 | tf_op jit(solution)/shard_map/ntu,nztxby,nbs->zuxsy/dot_general | solution.py:87
  82.5 0.9 broadcast_select_fusion.1
  83.5 0.7 all-gather.18.cloned.1.call-update
  84.2 38.7 %all-gather.16.cloned.1.call-done = f32[16,1,128,1,128]{4,2,3,1,0:T(8,128)} async-done(((f32[2,1,128,1,128]{4,2,3,1,0:T(8,128)}), f32[16,1,128,1,128]{4,2,3,1,0:T(8,128)}) %all-gather.16.cloned.1.call-update) | async-done | bytes 1048592 | tf_op jit(solution)/shard_map/all_gather | solution.py:10
  122.9 1.3 reduce.4
  124.2 39.9 %all-gather.18.cloned.1.call-done = f32[16,1,128,1,128]{4,2,3,1,0:T(8,128)} async-done(((f32[2,1,128,1,128]{4,2,3,1,0:T(8,128)}), f32[16,1,128,1,128]{4,2,3,1,0:T(8,128)}) %all-gather.18.cloned.1.call-update) | async-done | bytes 1048592 | tf_op jit(solution)/shard_map/all_gather | solution.py:10
  164.2 1.3 reduce.5
  165.5 0.7 broadcast_select_fusion.2
  166.1 0.7 broadcast_select_fusion.3
  166.9 0.5 all-gather.22.cloned.1.call-update
  167.7 0.3 all-gather.12.cloned.1.call-update
  168.1 199.6 %all-gather.20.cloned.1.call-done = bf16[128,1,128,256]{3,2,1,0:T(8,128)(2,1)} async-done(((bf16[2,1,128,256]{3,2,1,0:T(8,128)(2,1)}), bf16[128,1,128,256]{3,2,1,0:T(8,128)(2,1)}) %all-gather.20.cloned.1.call-update) | async-done | bytes 8388624 | tf_op jit(solution)/shard_map/all_gather | solution.py:10
  367.6 4.6 bitcast_reduce_fusion.1
  372.2 194.3 %all-gather.22.cloned.1.call-done = bf16[128,1,128,256]{3,2,1,0:T(8,128)(2,1)} async-done(((bf16[2,1,128,256]{3,2,1,0:T(8,128)(2,1)}), bf16[128,1,128,256]{3,2,1,0:T(8,128)(2,1)}) %all-gather.22.cloned.1.call-update) | async-done | bytes 8388624 | tf_op jit(solution)/shard_map/all_gather | solution.py:10
  566.6 4.6 bitcast_reduce_fusion
  571.2 2.3 gather_fusion.2
  573.6 2.3 gather_fusion.3
  576.0 0.3 fusion.32
  576.3 0.3 fusion.24
  576.7 0.4 convolution_subtract_fusion.6
  577.0 0.4 fusion.30
  577.5 0.3 convolution_add_fusion.6
  577.8 0.4 fusion.15
  578.2 0.4 fusion.27
  578.7 0.4 fusion.14
  580.2 0.4 fusion.42
  580.6 0.3 convolution_add_fusion.4
  580.9 0.4 fusion.13
  581.3 0.4 fusion.41
  581.7 0.4 fusion.12
  582.8 0.3 convolution_subtract_fusion.2
  583.1 0.4 fusion.46
  583.5 0.3 convolution_add_fusion.2
  583.8 0.4 fusion.11
  584.2 0.4 fusion.45
  584.6 0.4 fusion.10
  586.4 180.6 %all-gather.12.cloned.1.call-done = bf16[2,1,8192,256]{3,2,1,0:T(8,128)(2,1)} async-done(((bf16[2,1,128,256]{3,2,1,0:T(8,128)(2,1)}), bf16[2,1,8192,256]{3,2,1,0:T(8,128)(2,1)}) %all-gather.12.cloned.1.call-update) | async-done | bytes 8388624 | tf_op jit(solution)/shard_map/all_gather | solution.py:104
  767.0 1.3 constant_dynamic-slice_fusion
  768.2 0.3 fusion.75
  768.5 0.3 fusion.74
  768.9 0.3 fusion.9
  769.3 0.3 fusion.8
  769.7 1.2 fusion.20
  (45 shorter events, 4.3 us)
Async XLA Ops:
  6.5 64.7 %all-gather.14.cloned.1.call-start = ((), (), s32[]{:S(2)}) async-start(), calls=%async_computation.1 | async-start | bytes 4718592 | tf_op jit(solution)/shard_map/all_gather | solution.py:66
  8.4 114.5 %all-gather.16.cloned.1.call-start = ((), (), s32[]{:S(2)}) async-start(), calls=%async_computation.2 | async-start | bytes 1179648 | tf_op jit(solution)/shard_map/all_gather | solution.py:10
  83.4 80.8 %all-gather.18.cloned.1.call-start = ((), (), s32[]{:S(2)}) async-start(), calls=%async_computation.3 | async-start | bytes 1179648 | tf_op jit(solution)/shard_map/all_gather | solution.py:10
  84.1 283.5 %all-gather.20.cloned.1.call-start = ((), (), s32[]{:S(2)}) async-start(), calls=%async_computation.4 | async-start | bytes 8519680 | tf_op jit(solution)/shard_map/all_gather | solution.py:10
  166.1 1.6 copy-start
  166.9 399.7 %all-gather.22.cloned.1.call-start = ((), (), s32[]{:S(2)}) async-start(), calls=%async_computation.5 | async-start | bytes 8519680 | tf_op jit(solution)/shard_map/all_gather | solution.py:10
  167.5 599.5 %all-gather.12.cloned.1.call-start = ((), (), s32[]{:S(2)}) async-start(), calls=%async_computation | async-start | bytes 8519680 | tf_op jit(solution)/shard_map/all_gather | solution.py:104
Sparse Core Ops, SparseCore 0:
  9.4 61.7 all-gather.13
  83.5 39.3 all-gather.15
  125.0 39.0 all-gather.17
  168.5 199.0 all-gather.19
  372.0 194.5 all-gather.21
  570.8 196.1 all-gather.11
